TPU v7x, 1024 devices: a whole 4x4x32 slice. The times are simulated.
1024 devices in a mesh: dp: 4 (over y), expert: 32 (over z_hi, x, core), tensor: 8 (over z_lo).
Axes of the slice: x: 4, y: 4, z: 32 (z_hi: 4, z_lo: 8; z = z_hi * 8 + z_lo), core: 2. Of those that a mesh axis runs over, the one named last changes fastest.
Arguments:
- tokens: bfloat16 [1536, 4096], P(('dp', 'expert'), 'tensor'), may hold values from -60 to 60
- grad_out: bfloat16 [1536, 4096], P(('dp', 'expert'), 'tensor'), may hold values from -6 to 6
- route_ids: int32 [1536, 8], P(('dp', 'expert')), may hold values from 0 to 31, all different within a row; in each aligned block of 12 rows (0 to 11, 12 to 23, ...) at most 4 rows name the same one
- route_probs: float32 [1536, 8], P(('dp', 'expert')), may hold values from 0.05 to 1
- w_gate: bfloat16 [32, 4096, 1536], P('expert', None, 'tensor'), may hold values from -0.09375 to 0.09375
- w_up: bfloat16 [32, 4096, 1536], P('expert', None, 'tensor'), may hold values from -0.09375 to 0.09375
- w_down: bfloat16 [32, 1536, 4096], P('expert', 'tensor'), may hold values from -0.15625 to 0.15625
Outputs:
- mixed: bfloat16 [1536, 4096], P(('dp', 'expert'), 'tensor')
- grad_tokens: bfloat16 [1536, 4096], P(('dp', 'expert'), 'tensor')
- grad_down: float32 [32, 1536, 4096], P('expert', 'tensor', 'dp')
Inputs may be any that keep to these rules, and one draw needn't show every extreme that they name: `route_ids`: each row names 8 different experts; in the rows of one device (aligned blocks of 12 rows) no expert is named more than 4 times, a bound that some block reaches.
All inputs are finite; a program needn't handle non-finite values. Where the computation divides by a largest or mean magnitude, that divisor is 1e-20 or more.
Results may differ from a plain program's by a relative error of at most 0.015.
Values may be sent and summed in bfloat16 or wider, within the bound.
A program may use at most 64 MiB of HBM per device.

v0:
```python
import jax
import jax.numpy as jnp
from jax import lax
from jax.sharding import PartitionSpec as P

EXPERTS = 32
TOPK = 8
CAP = 4


amax_target = 4.0
eps_scale = 1e-05


def in_one_piece(arrays, axis, split_dim, concat_dim, along):
    ends, at = ([], 0)
    for a in arrays[:-1]:
        at += a.shape[along]
        ends.append(at)
    both = jnp.concatenate(arrays, axis=along)
    return tuple(
        jnp.split(
            lax.all_to_all(both, axis, split_axis=split_dim, concat_axis=concat_dim, tiled=True),
            ends,
            axis=along,
        )
    )


def in_one_piece_2(arrays, axis, dim, along):
    widths = [a.shape[along] for a in arrays]
    both = jnp.concatenate(arrays, axis=along)
    out = lax.all_gather(both, axis, axis=dim, tiled=True)
    return tuple(jnp.split(out, [sum(widths[:k]) for k in range(1, len(widths))], axis=along))


def in_one_piece_3(arrays, axis, dim, along):
    ends, at = ([], 0)
    for a in arrays[:-1]:
        at += a.shape[along]
        ends.append(at)
    both = jnp.concatenate(arrays, axis=along)
    return tuple(
        jnp.split(lax.psum_scatter(both, axis, scatter_dimension=dim, tiled=True), ends, axis=along)
    )


def split_up(value, dim, size):
    before, after = (value.shape[:dim], value.shape[dim + 1 :])
    return jnp.moveaxis(value.reshape(*before, size, -1, *after), dim, 0)


def summed_on_arrival(value, axis, dim):
    size = lax.axis_size(axis)
    pieces = lax.all_to_all(split_up(value, dim, size), axis, 0, 0, tiled=True)
    return jnp.sum(pieces.astype(jnp.float32), axis=0)


def slot_layout(route_ids):
    flat_ids = route_ids.reshape(-1)
    onehot = (flat_ids[:, None] == jnp.arange(EXPERTS, dtype=jnp.int32)[None, :]).astype(jnp.int32)
    slot_rank = jnp.sum(onehot * (jnp.cumsum(onehot, axis=0) - 1), axis=1)
    slot_index = flat_ids * CAP + slot_rank
    pair_count = flat_ids.shape[0]
    slot_pair = (
        jnp.zeros((EXPERTS * CAP,), jnp.int32)
        .at[slot_index]
        .set(jnp.arange(pair_count, dtype=jnp.int32))
    )
    slot_live = (
        jnp.zeros((EXPERTS * CAP,), jnp.float32)
        .at[slot_index]
        .set(jnp.ones((pair_count,), jnp.float32))
    )
    return (slot_index, slot_pair, slot_live)


def pick_rows(source, row_index, slot_live):
    picked = source[row_index]
    return jnp.where(slot_live[:, None] > 0, picked, jnp.zeros_like(picked))


def scale_rows(raw_rows):
    magnitude = jnp.max(jnp.abs(raw_rows.astype(jnp.float32)), axis=1)
    factor = amax_target / (magnitude + eps_scale)
    return ((raw_rows.astype(jnp.float32) * factor[:, None]).astype(jnp.bfloat16), factor)


def on_device(tokens, grad_out, route_ids, route_probs, w_gate, w_up, w_down):
    tok_rows = tokens.shape[0]
    exp_local = w_gate.shape[0]
    n_expert = lax.axis_size("expert")
    slot_index, slot_pair, slot_live = slot_layout(route_ids)
    token_of_slot = slot_pair // TOPK
    send_x = pick_rows(tokens, token_of_slot, slot_live)
    weighted = route_probs[:, :, None] * grad_out.astype(jnp.float32)[:, None, :]
    send_dy = pick_rows(
        weighted.astype(jnp.bfloat16).reshape(tok_rows * TOPK, grad_out.shape[1]),
        slot_pair,
        slot_live,
    )
    recv_x, recv_dy = in_one_piece((send_x, send_dy), "expert", 0, 0, 1)
    raw_x, dy_rows = in_one_piece_2((recv_x, recv_dy), "tensor", 1, 0)
    scaled, factor = scale_rows(raw_x)
    slot_rows = n_expert * CAP

    def by_expert(rows):
        last = rows.shape[-1]
        return (
            rows.reshape(n_expert, exp_local, CAP, last)
            .transpose(1, 0, 2, 3)
            .reshape(exp_local, slot_rows, last)
        )

    def by_source(rows):
        last = rows.shape[-1]
        return (
            rows.reshape(exp_local, n_expert, CAP, last)
            .transpose(1, 0, 2, 3)
            .reshape(n_expert * exp_local * CAP, last)
        )

    x_slots = by_expert(scaled)
    dy_slots = by_expert(dy_rows)
    row_factor = by_expert(factor.reshape(-1, 1))
    gate = jnp.einsum("erd,edf->erf", x_slots, w_gate, preferred_element_type=jnp.float32)
    upval = jnp.einsum("erd,edf->erf", x_slots, w_up, preferred_element_type=jnp.float32)
    sigma = jax.nn.sigmoid(gate)
    active = gate * sigma
    hidden = (active * upval).astype(jnp.bfloat16)
    grad_hidden = jnp.einsum("erd,efd->erf", dy_slots, w_down, preferred_element_type=jnp.float32)
    grad_gate = (grad_hidden * upval * sigma * (1.0 + gate * (1.0 - sigma))).astype(jnp.bfloat16)
    grad_up = (grad_hidden * active).astype(jnp.bfloat16)
    dx_part = jnp.einsum("erf,edf->erd", grad_gate, w_gate, preferred_element_type=jnp.float32)
    dx_part = dx_part + jnp.einsum(
        "erf,edf->erd", grad_up, w_up, preferred_element_type=jnp.float32
    )
    dx_part = dx_part * row_factor
    out_part = jnp.einsum("erf,efd->erd", hidden, w_down, preferred_element_type=jnp.float32)
    summed_out, summed_dx = tuple(
        (
            part.astype(jnp.float32)
            for part in in_one_piece_3(
                (out_part.astype(jnp.bfloat16), dx_part.astype(jnp.bfloat16)), "tensor", 2, 0
            )
        )
    )
    send_out = by_source(summed_out.astype(jnp.bfloat16))
    send_dx = by_source(summed_dx.astype(jnp.bfloat16))
    back_out, back_dx = in_one_piece((send_out, send_dx), "expert", 0, 0, 1)
    local_width = back_out.shape[1]
    pair_out = back_out[slot_index].astype(jnp.float32).reshape(tok_rows, TOPK, local_width)
    mixed = jnp.sum(pair_out * route_probs[:, :, None], axis=1).astype(jnp.bfloat16)
    pair_dx = back_dx[slot_index].astype(jnp.float32).reshape(tok_rows, TOPK, local_width)
    grad_tokens = jnp.sum(pair_dx, axis=1).astype(jnp.bfloat16)
    weight_term = jnp.einsum("erf,erd->efd", hidden, dy_slots, preferred_element_type=jnp.float32)
    grad_down = summed_on_arrival(weight_term.astype(jnp.bfloat16), "dp", 2)
    return (mixed, grad_tokens, grad_down)


def solution(mesh):
    return jax.shard_map(
        on_device,
        mesh=mesh,
        in_specs=(
            P(("dp", "expert"), "tensor"),
            P(("dp", "expert"), "tensor"),
            P(("dp", "expert"), None),
            P(("dp", "expert"), None),
            P("expert", None, "tensor"),
            P("expert", None, "tensor"),
            P("expert", "tensor", None),
        ),
        out_specs=(
            P(("dp", "expert"), "tensor"),
            P(("dp", "expert"), "tensor"),
            P("expert", "tensor", "dp"),
        ),
        check_vma=False,
    )
```

profile of v0, /device:TPU:24, one launch (start us, length us, event | category | flops | bytes accessed | tf_op | source)
XLA Modules:
  0.0 309.8 jit_solution(9815980679502483118)
XLA Ops:
  7.2 0.8 broadcast_multiply_fusion
  8.0 0.8 copy.19
  9.0 0.8 copy.20
  9.9 0.7 convert_element_type.66
  11.1 0.9 scatter_custom_fusion.1
  12.0 0.9 scatter_custom_fusion
  13.1 0.8 gather_fusion.1
  14.0 0.8 gather_fusion
  15.2 65.1 %all_to_all.23 = bf16[32,4,1024]{2,1,0:T(4,128)(2,1)} all-to-all(bf16[32,4,1024]{2,1,0:T(4,128)(2,1)S(1)} %pad_maximum_fusion.1), channel_id=1, replica_groups=mesh['dp'=4,'expert'=32,'tensor'=8] {'expert'}, dimensions={0} | all-to-all | bytes 524288 | tf_op jit(solution)/shard_map/all_to_all | solution.py:23
  80.3 1.0 all_to_all.16
  81.3 0.7 pad_maximum_fusion.2
  82.1 73.8 %all-gather.2.cloned.1.call-done = bf16[256,4096]{1,0:T(8,128)(2,1)} async-done(((bf16[256,512]{1,0:T(8,128)(2,1)}), bf16[256,4096]{1,0:T(8,128)(2,1)}) %all-gather.2.cloned.1.call-update) | async-done | bytes 2097168 | tf_op jit(solution)/shard_map/all_gather | solution.py:33
  156.0 1.6 fusion.4
  157.6 1.9 fusion.14
  159.5 0.7 multiply_convert_fusion.2
  160.2 0.7 copy-done.2
  161.4 0.6 fusion.6
  163.1 1.5 pad_maximum_fusion
  164.6 3.0 convolution_convert_fusion
  167.6 2.9 reshape.145
  170.5 1.6 copy.24
  172.1 4.8 %all-to-all-start.2 = ((bf16[4,1,192,1024]{3,2,1,0:T(8,128)(2,1)}), bf16[4,1,192,1024]{3,2,1,0:T(8,128)(2,1)S(1)}, u32[]{:S(2)}, u32[]{:S(2)}) async-start(bf16[4,1,192,1024]{3,2,1,0:T(8,128)(2,1)} %bitcast.44), calls=%async_computation.3 | async-start | bytes 3145728 | tf_op jit(solution)/shard_map/all_to_all | solution.py:55
  176.9 67.5 %reduce-scatter.2.cloned.1.call-done = bf16[2,128,512]{2,1,0:T(8,128)(2,1)} async-done(((bf16[2,128,4096]{2,1,0:T(8,128)(2,1)}), bf16[2,128,512]{2,1,0:T(8,128)(2,1)}) %reduce-scatter.2.cloned.1.call-update) | async-done | bytes 262160 | tf_op jit(solution)/shard_map/reduce_scatter | solution.py:44
  244.4 1.0 fusion.34
  245.4 0.8 pad_maximum_fusion.3
  246.3 19.5 %all-to-all-start.1 = ((bf16[32,4,1024]{2,1,0:T(4,128)(2,1)}), bf16[32,4,1024]{2,1,0:T(4,128)(2,1)S(1)}, u32[]{:S(2)}, u32[]{:S(2)}) async-start(bf16[32,4,1024]{2,1,0:T(4,128)(2,1)} %pad_maximum_fusion.3), calls=%async_computation.2 | async-start | bytes 524288 | tf_op jit(solution)/shard_map/all_to_all | solution.py:23
  265.8 1.2 convert_reduce_fusion
  267.0 33.0 %all-to-all-done.1 = bf16[32,4,1024]{2,1,0:T(4,128)(2,1)S(1)} async-done(((bf16[32,4,1024]{2,1,0:T(4,128)(2,1)}), bf16[32,4,1024]{2,1,0:T(4,128)(2,1)S(1)}, u32[]{:S(2)}, u32[]{:S(2)}) %all-to-all-start.1) | async-done | bytes 262176 | tf_op jit(solution)/shard_map/all_to_all | solution.py:23
  300.0 0.8 gather_fusion.3
  300.8 0.7 bitcast_reduce_fusion
  301.5 0.8 gather_fusion.2
  302.3 0.7 fusion.20
  (43 shorter events, 3.2 us)
Async XLA Ops:
  7.2 152.3 %copy-start = (bf16[1,4096,192]{1,2,0:T(8,128)(2,1)S(1)}, bf16[1,4096,192]{1,2,0:T(8,128)(2,1)}, u32[]{:S(2)}) copy-start(bf16[1,4096,192]{1,2,0:T(8,128)(2,1)} %param.12) | copy-start | bytes 4718596
  7.2 6.8 %copy-start.1 = (bf16[12,512]{1,0:T(8,128)(2,1)S(1)}, bf16[12,512]{1,0:T(8,128)(2,1)}, u32[]{:S(2)}) copy-start(bf16[12,512]{1,0:T(8,128)(2,1)} %param.7) | copy-start | bytes 36868
  7.2 148.8 %all-gather.2.cloned.1.call-start = ((), (), s32[]{:S(2)}) async-start(), calls=%async_computation.4 | async-start | bytes 2359296 | tf_op jit(solution)/shard_map/all_gather | solution.py:33
  15.1 142.5 %copy-start.4 = (bf16[1,4096,192]{1,2,0:T(8,128)(2,1)S(1)}, bf16[1,4096,192]{1,2,0:T(8,128)(2,1)}, u32[]{:S(2)}) copy-start(bf16[1,4096,192]{1,2,0:T(8,128)(2,1)} %param.11) | copy-start | bytes 4718596
  82.1 162.3 %reduce-scatter.2.cloned.1.call-start = ((), (), s32[]{:S(2)}) async-start(), calls=%async_computation.5 | async-start | bytes 2359296 | tf_op jit(solution)/shard_map/reduce_scatter | solution.py:44
  156.0 3.6 %copy-start.3 = (bf16[256,4096]{1,0:T(8,128)(2,1)S(1)}, bf16[256,4096]{1,0:T(8,128)(2,1)}, u32[]{:S(2)}) copy-start(bf16[256,4096]{1,0:T(8,128)(2,1)} %all-gather.2.cloned.1.call-done) | copy-start | bytes 6291460
  159.5 1.4 copy-start.2
  172.1 74.2 %all-to-all-start.2 = ((bf16[4,1,192,1024]{3,2,1,0:T(8,128)(2,1)}), bf16[4,1,192,1024]{3,2,1,0:T(8,128)(2,1)S(1)}, u32[]{:S(2)}, u32[]{:S(2)}) async-start(bf16[4,1,192,1024]{3,2,1,0:T(8,128)(2,1)} %bitcast.44), calls=%async_computation.3 | async-start | bytes 3145728 | tf_op jit(solution)/shard_map/all_to_all | solution.py:55
  246.3 53.7 %all-to-all-start.1 = ((bf16[32,4,1024]{2,1,0:T(4,128)(2,1)}), bf16[32,4,1024]{2,1,0:T(4,128)(2,1)S(1)}, u32[]{:S(2)}, u32[]{:S(2)}) async-start(bf16[32,4,1024]{2,1,0:T(4,128)(2,1)} %pad_maximum_fusion.3), calls=%async_computation.2 | async-start | bytes 524288 | tf_op jit(solution)/shard_map/all_to_all | solution.py:23
Sparse Core Ops, SparseCore 0:
  82.2 73.6 all-gather.1
  164.7 79.5 reduce-scatter.1
where the time goes:
time: 312 us; the launch traced here: 310 us
  waiting for transfers between devices  174 us (56%)
  blocking collectives  65.1 us (21%)
  starting transfers between devices  24.4 us (8%)
  local copies, waits for them, and re-layouts  14.5 us (5%)
  between operations  14.3 us (5%)
  other arithmetic  9.61 us (3%)
  matrix products  7.62 us (2%)
    all_gather x1, waiting for transfers between devices, in_one_piece_2(): out = lax.all_gather(both, axis, axis=dim, tiled=True)  73.8 us
    reduce_scatter x1, waiting for transfers between devices, in_one_piece_3(): lax.psum_scatter(both, axis, scatter_dimension=dim, tiled=True)  67.5 us
    all_to_all x1, blocking collectives, in_one_piece(): lax.all_to_all(both, axis, split_axis=split_dim, concat_axis=concat_dim,...  65.1 us
    all_to_all x1, waiting for transfers between devices, in_one_piece(): lax.all_to_all(both, axis, split_axis=split_dim, concat_axis=concat_dim,...  33 us
    all_to_all x1, starting transfers between devices, in_one_piece(): lax.all_to_all(both, axis, split_axis=split_dim, concat_axis=concat_dim,...  19.5 us
  transfers between devices with their start and end apart: 4, of which 3 were waited for; matrix products, arithmetic and copies ran while one was open for 3% of the time, Pallas kernels for 0%

commit v1 on v0

v1 whole, which is shorter than its diff:
```python
import jax
import jax.numpy as jnp
from jax import lax
from jax.sharding import PartitionSpec as P

EXPERTS = 32
amax_target = 4.0
eps_scale = 1e-05
PLANE = ("expert", "tensor")
bf16, f32 = jnp.bfloat16, jnp.float32


def on_device(tokens, grad_out, route_ids, route_probs, w_gate, w_up, w_down):
    rows, width = tokens.shape
    n_e, n_t = lax.axis_size("expert"), lax.axis_size("tensor")
    me = lax.axis_index("expert")
    both = jnp.stack([tokens, grad_out])
    whole = lax.all_gather(both, PLANE, axis=0, tiled=False)
    whole = whole.reshape(n_e, n_t, 2, rows, width).transpose(2, 0, 3, 1, 4)
    whole = whole.reshape(2, n_e * rows, n_t * width)
    x, g = whole[0], whole[1]
    dense = jnp.sum(
        jnp.where(
            route_ids[:, :, None] == jnp.arange(EXPERTS, dtype=jnp.int32), route_probs[:, :, None], 0.0
        ),
        axis=1,
    )
    probs = lax.all_gather(dense, "expert", axis=0, tiled=True)
    prob = lax.dynamic_slice_in_dim(probs, me, 1, axis=1)
    live = prob > 0
    magnitude = jnp.max(jnp.abs(x), axis=1, keepdims=True).astype(f32)
    factor = amax_target / (magnitude + eps_scale)
    wg, wu, wd = w_gate[0], w_up[0], w_down[0]
    gate = factor * jnp.dot(x, wg, preferred_element_type=f32)
    upval = factor * jnp.dot(x, wu, preferred_element_type=f32)
    sigma = jax.nn.sigmoid(gate)
    active = gate * sigma
    hidden = (jnp.where(live, prob, 0.0) * active * upval).astype(bf16)
    gh = jnp.einsum("rd,fd->rf", g, wd, preferred_element_type=f32) * (prob * factor)
    gg = (gh * upval * sigma * (1.0 + gate * (1.0 - sigma))).astype(bf16)
    gu = (gh * active).astype(bf16)
    dx = jnp.einsum("rf,df->rd", gg, wg, preferred_element_type=f32)
    dx = dx + jnp.einsum("rf,df->rd", gu, wu, preferred_element_type=f32)
    out = jnp.dot(hidden, wd, preferred_element_type=f32)
    parts = jnp.stack([out.astype(bf16), dx.astype(bf16)])
    parts = parts.reshape(2, n_e, rows, n_t, width).transpose(1, 3, 0, 2, 4)
    parts = parts.reshape(n_e * n_t, 2 * rows, width)
    mine = lax.psum_scatter(parts, PLANE, scatter_dimension=0, tiled=False)
    mixed, grad_tokens = mine[:rows], mine[rows:]
    term = jnp.einsum("rf,rd->fd", hidden, g, preferred_element_type=f32).astype(bf16)
    n_dp = lax.axis_size("dp")
    pieces = jnp.moveaxis(term.reshape(term.shape[0], n_dp, -1), 1, 0)
    pieces = lax.all_to_all(pieces, "dp", 0, 0, tiled=True)
    grad_down = jnp.sum(pieces.astype(f32), axis=0)[None]
    return (mixed, grad_tokens, grad_down)


def solution(mesh):
    return jax.shard_map(
        on_device,
        mesh=mesh,
        in_specs=(
            P(("dp", "expert"), "tensor"),
            P(("dp", "expert"), "tensor"),
            P(("dp", "expert"), None),
            P(("dp", "expert"), None),
            P("expert", None, "tensor"),
            P("expert", None, "tensor"),
            P("expert", "tensor", None),
        ),
        out_specs=(
            P(("dp", "expert"), "tensor"),
            P(("dp", "expert"), "tensor"),
            P("expert", "tensor", "dp"),
        ),
        check_vma=False,
    )
```

time: 312 us -> 2370 us (7.60)
  the two profiles are of different devices: /device:TPU:24 before, /device:TPU:10 now
where the time goes in v1:
time: 2370 us
  waiting for transfers between devices  2200 us (93%)
  blocking collectives  102 us (4%)
  local copies, waits for them, and re-layouts  31.8 us (1%)
    reduce_scatter x1, waiting for transfers between devices, on_device(): mine = lax.psum_scatter(parts, PLANE, scatter_dimension=0, tiled=False)  1540 us
    all_gather x1, waiting for transfers between devices, on_device(): whole = lax.all_gather(both, PLANE, axis=0, tiled=False)  661 us
    all_gather x1, blocking collectives, on_device(): probs = lax.all_gather(dense, 'expert', axis=0, tiled=True)  78.6 us
  transfers between devices with their start and end apart: 2, of which 2 were waited for; matrix products, arithmetic and copies ran while one was open for 0% of the time, Pallas kernels for 0%

profile of v1, /device:TPU:10, one launch (start us, length us, event | category | flops | bytes accessed | tf_op | source)
XLA Modules:
  0.0 2367.7 jit_solution(5829210167929026241)
XLA Ops:
  7.2 1.5 pad_maximum_fusion.1
  8.8 0.8 copy.33
  9.5 0.8 copy.34
  10.4 78.6 %all-gather.1 = f32[32,12,32]{2,1,0:T(8,128)S(1)} all-gather(f32[1,12,32]{2,1,0:T(8,128)S(1)} %bitcast.79), channel_id=1, replica_groups=mesh['dp'=4,'expert'=32,'tensor'=8] {'expert'}, dimensions={0}, use_global_device_ids=true | all-gather | bytes 50688 | tf_op jit(solution)/shard_map/all_gather | solution.py:28
  89.0 661.1 %all-gather.4.cloned.1.call-done = bf16[512,12,512]{2,1,0:T(8,128)(2,1)} async-done(((bf16[2,12,512]{2,1,0:T(8,128)(2,1)}), bf16[512,12,512]{2,1,0:T(8,128)(2,1)}) %all-gather.4.cloned.1.call-update) | async-done | bytes 6291472 | tf_op jit(solution)/shard_map/all_gather | solution.py:18
  750.1 10.7 copy.49
  760.9 4.8 fusion.25
  765.6 0.1 div.26
  765.8 0.1 div.29
  765.9 3.5 copy.45
  769.4 1.5 copy.43
  770.9 0.3 fusion.20
  771.1 0.8 copy-done.6
  771.9 1.2 fusion.10
  773.1 1.2 multiply_convert_fusion.2
  774.3 0.2 copy-done.5
  774.5 1.0 convolution_convert_fusion
  775.5 1.4 copy.44
  777.0 1.2 fusion.16
  778.2 1.1 fusion.6
  779.2 1.1 add_convert_fusion
  780.3 1.4 copy.46
  781.7 0.8 pad_maximum_fusion
  782.5 0.8 copy.41
  783.3 6.3 copy.39
  789.7 1.9 copy-done.3
  791.5 1.0 convolution_convert_fusion.1
  792.5 0.1 copy.50
  792.7 23.7 %all_to_all.5 = bf16[4,192,1024]{2,1,0:T(8,128)(2,1)S(1)} all-to-all(bf16[4,192,1024]{2,1,0:T(8,128)(2,1)S(1)} %bitcast.75), channel_id=1, replica_groups=mesh['dp'=4,'expert'=32,'tensor'=8] {'dp'}, dimensions={0} | all-to-all | bytes 3145728 | tf_op jit(solution)/shard_map/all_to_all | solution.py:53
  816.4 1.2 convert_reduce_fusion
  817.5 1541.9 %reduce-scatter.2.cloned.1.call-done = bf16[1,24,512]{2,1,0:T(8,128)(2,1)} async-done(((bf16[256,24,512]{2,1,0:T(8,128)(2,1)}), bf16[1,24,512]{2,1,0:T(8,128)(2,1)}) %reduce-scatter.2.cloned.1.call-update) | async-done | bytes 24592 | tf_op jit(solution)/shard_map/reduce_scatter | solution.py:48
  2359.5 1.4 slice_bitcast_fusion
  (18 shorter events, 0.3 us)
Async XLA Ops:
  7.2 766.0 %copy-start = (bf16[1,4096,192]{1,2,0:T(8,128)(2,1)S(1)}, bf16[1,4096,192]{1,2,0:T(8,128)(2,1)}, u32[]{:S(2)}) copy-start(bf16[1,4096,192]{1,2,0:T(8,128)(2,1)} %param.12) | copy-start | bytes 4718596
  7.2 743.0 %all-gather.4.cloned.1.call-start = ((), (), s32[]{:S(2)}) async-start(), calls=%async_computation.3 | async-start | bytes 8421376 | tf_op jit(solution)/shard_map/all_gather | solution.py:18
  8.7 2350.7 %reduce-scatter.2.cloned.1.call-start = ((), (), s32[]{:S(2)}) async-start(), calls=%async_computation.2 | async-start | bytes 6316032 | tf_op jit(solution)/shard_map/reduce_scatter | solution.py:48
  765.9 3.5 copy-start.4
  769.4 7.6 copy-start.2
  769.4 2.5 copy-start.6
  773.1 1.4 copy-start.5
  789.6 1.9 copy-start.3
  792.5 1568.4 %copy-start.1 = (bf16[1,4096,192]{1,2,0:T(8,128)(2,1)S(1)}, bf16[1,4096,192]{1,2,0:T(8,128)(2,1)}, u32[]{:S(2)}) copy-start(bf16[1,4096,192]{1,2,0:T(8,128)(2,1)} %param.12) | copy-start | bytes 4718596
Sparse Core Ops, SparseCore 0:
  11.3 738.7 all-gather.3
  789.8 1569.6 reduce-scatter.1

commit v2 on v1

v2 whole, which is shorter than its diff:
```python
import functools

import jax
import jax.numpy as jnp
import numpy as np
from jax import lax
from jax.experimental import pallas as pl
from jax.experimental.pallas import tpu as pltpu
from jax.sharding import PartitionSpec as P

EXPERTS = 32
AMAX_TARGET = 4.0
EPS_SCALE = 1e-05
LANES = 128
NX, NC = 4, 2
P_ROWS = 16
bf16, f32 = jnp.bfloat16, jnp.float32
MESH = pl.DeviceIdType.MESH
VMEM_BYTES = 56 * 1024 * 1024


def mm(a, b):
    return jnp.dot(a, b, preferred_element_type=f32)


def mm_nt(a, b):
    return lax.dot_general(a, b, (((1,), (1,)), ((), ())), preferred_element_type=f32)


def mm_tn(a, b):
    return lax.dot_general(a, b, (((0,), (0,)), ((), ())), preferred_element_type=f32)


def kernel(
    ny, nh, nz, tok, wid,
    blk, perm, permt, permp, wg_h, wu_h, wd_h,
    out, gd,
    hbuf, pb, xb, wg, wu, wd, gate_acc, up_acc, gh_acc, amax, hp, gg, gu,
    cb, sb, xr1, xl1, xr2, xl2, zs, zr, zl_buf, wt, yr1, yl1, yr2, yl2, fp, hb2,
    w_sem, h_s, h_r, p_s, p_r, z_s, z_r, xa_s, xa_r, xb_s, xb_r, sib_s, sib_r,
    cs_s, cs_r, x1_s, x1_r, x2_s, x2_r, zz_s, zz_r, y_s, y_r, f_s, f_r,
):
    half = nz // 2
    q_n = wid // LANES
    rows = nh * tok
    every = NX * NC * rows
    packed = q_n * tok
    y, e, z = lax.axis_index("dp"), lax.axis_index("expert"), lax.axis_index("tensor")
    c = lax.rem(e, NC)
    x = lax.rem(e // NC, NX)
    h = e // (NC * NX)

    def eid(h_, x_, c_):
        return (h_ * NX + x_) * NC + c_

    x_right, x_left, x_far = (lax.rem(x + k, NX) for k in (1, 3, 2))
    d_xr, d_xl, d_xf = ((y, eid(h, k, c), z) for k in (x_right, x_left, x_far))
    d_sib = (y, eid(h, x, 1 - c), z)
    d_zr = (y, eid(lax.rem(h + (z + 1) // nz, nh), x, c), lax.rem(z + 1, nz))
    d_zl = (
        y,
        eid(lax.rem(h + nh - 1 + (z + nz - 1) // nz, nh), x, c),
        lax.rem(z + nz - 1, nz),
    )
    d_h = [(y, eid(lax.rem(h + k, nh), x, c), z) for k in range(1, nh)]
    d_yr, d_yl = (lax.rem(y + 1, ny), e, z), (lax.rem(y + ny - 1, ny), e, z)

    def rdma(src, dst, s, r, dev):
        return pltpu.make_async_remote_copy(
            src_ref=src, dst_ref=dst, send_sem=s, recv_sem=r, device_id=dev, device_id_type=MESH
        )

    loads = [
        pltpu.make_async_copy(a, b, w_sem.at[i])
        for i, (a, b) in enumerate(((wg_h, wg), (wu_h, wu), (wd_h, wd)))
    ]
    for load in loads:
        load.start()

    partners = [d_xr, d_xl, d_xf, d_sib, d_zr, d_zl, *d_h]
    if ny > 1:
        partners += [d_yr, d_yl]
    barrier = pltpu.get_barrier_semaphore()
    for dev in partners:
        pl.semaphore_signal(barrier, inc=1, device_id=dev, device_id_type=MESH)
    pl.semaphore_wait(barrier, len(partners))

    h_out = [
        rdma(blk, hbuf.at[h], h_s.at[k], h_r.at[k], dev) for k, dev in enumerate(d_h)
    ]
    for cp in h_out:
        cp.start()
    hbuf[pl.ds(h, 1)] = blk[...][None]
    gate_acc[...] = jnp.zeros_like(gate_acc)
    up_acc[...] = jnp.zeros_like(up_acc)
    gh_acc[...] = jnp.zeros_like(gh_acc)
    amax[...] = jnp.zeros_like(amax)
    zr[0, 1] = jnp.zeros_like(zr[0, 1])
    zl_buf[0, 0] = jnp.zeros_like(zl_buf[0, 0])
    for cp in h_out:
        cp.wait_recv()
    for a in range(2):
        block = hbuf[:, a * packed : (a + 1) * packed, :].reshape(nh * packed, LANES)
        spread = mm(perm[...], block).astype(bf16)
        for q in range(q_n):
            xb[z, a, x, c, :, q * LANES : (q + 1) * LANES] = spread[q * rows : (q + 1) * rows]
    pieces = hbuf[:, 2 * packed :, :].reshape(nh * P_ROWS, LANES)
    pb[x, c] = mm(permp[...], pieces).astype(bf16)

    def at_step(t):
        d = (t + 1) // 2
        return lax.rem(z + d * (1 - 2 * lax.rem(t, 2)) + nz, nz)

    def z_copy(way, d, split):
        s = lax.rem(z + (d if way else -d) + nz, nz)
        ref = xb.at[s, way, x, c] if split else xb.at[s, :, x, c]
        return rdma(ref, ref, z_s.at[way, d], z_r.at[way, d], d_zl if way else d_zr)

    def z_send(way, d):
        @pl.when(d < half - 1)
        def _():
            z_copy(way, d, False).start()

        @pl.when(d == half - 1)
        def _():
            z_copy(way, d, True).start()

    def xa_copy(t, way):
        ref = xb.at[at_step(t), :, x, c]
        return rdma(ref, ref, xa_s.at[way, t], xa_r.at[way, t], d_xl if way else d_xr)

    def xb_copy(t, way):
        ref = xb.at[at_step(t), way, x_right if way else x_left, c]
        return rdma(ref, ref, xb_s.at[way, t], xb_r.at[way, t], d_xl if way else d_xr)

    def sib_copy(t):
        ref = xb.at[at_step(t), :, :, c]
        return rdma(ref, ref, sib_s.at[t], sib_r.at[t], d_sib)

    def p_copy(k):
        ref = pb.at[x, c]
        return rdma(ref, ref, p_s.at[k], p_r.at[k], (d_xr, d_xl, d_xf)[k])

    def p_sib():
        ref = pb.at[:, c]
        return rdma(ref, ref, p_s.at[3], p_r.at[3], d_sib)

    def gather_step(t, carry):
        @pl.when(t < nz)
        def _():
            d = (t + 1) // 2
            odd = lax.rem(t, 2)

            @pl.when(t == 0)
            def _():
                z_send(0, t)
                z_send(1, t)

            @pl.when((odd == 1) & (t < nz - 1))
            def _():
                z_copy(0, d - 1, False).wait_recv()
                z_send(0, d)

            @pl.when((odd == 0) & (t > 0))
            def _():
                z_copy(1, d - 1, False).wait_recv()
                z_send(1, d)

            @pl.when(t == nz - 1)
            def _():
                z_copy(0, half - 1, True).wait_recv()
                z_copy(1, half - 1, True).wait_recv()

            for way in range(2):
                xa_copy(t, way).start()

            @pl.when(t == 0)
            def _():
                for k in range(3):
                    p_copy(k).start()

        @pl.when((t >= 1) & (t < nz + 1))
        def _():
            for way in range(2):
                xa_copy(t - 1, way).wait_recv()
                xb_copy(t - 1, way).start()

        @pl.when((t >= 2) & (t < nz + 2))
        def _():
            for way in range(2):
                xb_copy(t - 2, way).wait_recv()
            sib_copy(t - 2).start()

            @pl.when(t == 2)
            def _():
                for k in range(3):
                    p_copy(k).wait_recv()
                p_sib().start()

        @pl.when(t == 3)
        def _():
            for load in loads:
                load.wait()

        @pl.when(t >= 3)
        def _():
            sib_copy(t - 3).wait_recv()
            s = at_step(t - 3)
            cols = pl.ds(pl.multiple_of(s * wid, wid), wid)
            x_rows = xb[s, 0].reshape(every, wid)
            gate_acc[...] += mm(x_rows, wg[cols, :])
            up_acc[...] += mm(x_rows, wu[cols, :])
            gh_acc[...] += mm_nt(xb[s, 1].reshape(every, wid), wd[:, cols])
            size = jnp.abs(x_rows.astype(f32))
            top = amax[...]
            for q in range(q_n):
                top = jnp.maximum(top, size[:, q * LANES : (q + 1) * LANES])
            amax[...] = top

        return carry

    lax.fori_loop(0, nz + 3, gather_step, 0)

    p_sib().wait_recv()
    lane = lax.broadcasted_iota(jnp.int32, (every, LANES), 1)
    mine = (lane == e) | (lane == e + EXPERTS) | (lane == e + 2 * EXPERTS)
    prob = jnp.sum(
        jnp.where(mine, pb[...].reshape(every, LANES).astype(f32), 0.0), axis=1, keepdims=True
    )
    factor = AMAX_TARGET / (jnp.max(amax[...], axis=1, keepdims=True) + EPS_SCALE)
    gate = gate_acc[...] * factor
    upval = up_acc[...] * factor
    sigma = jax.nn.sigmoid(gate)
    active = gate * sigma
    grad = gh_acc[...] * (prob * factor)
    hp[...] = (prob * active * upval).astype(bf16)
    gg[...] = (grad * upval * sigma * (1.0 + gate * (1.0 - sigma))).astype(bf16)
    gu[...] = (grad * active).astype(bf16)

    def y_term(dest):
        for k in range(2):
            wt[dest, k] = mm_tn(hp[...], xb[2 * dest + k, 1].reshape(every, wid)).astype(bf16)

    y_far, y_right, y_left = (lax.rem(y + k, ny) for k in (2, 1, 3))

    def y1_copy(way):
        src, dst = wt.at[y_far, way], (yl1 if way else yr1)
        return rdma(src, dst, y_s.at[way], y_r.at[way], d_yl if way else d_yr)

    def y2_copy(way):
        src, dst = wt.at[y_left if way else y_right], (yl2 if way else yr2)
        return rdma(src, dst, y_s.at[2 + way], y_r.at[2 + way], d_yl if way else d_yr)

    def dest_of(k):
        odd = lax.rem(k, 2)
        off = jnp.where(odd == 1, half - (k + 1) // 2, k // 2 - half)
        return lax.rem(z + off + nz, nz)

    def cs_copy(k):
        return rdma(cb.at[k, :, :, 1 - c], sb.at[k], cs_s.at[k], cs_r.at[k], d_sib)

    def x1_copy(k, way):
        dst = (xl1 if way else xr1).at[k]
        return rdma(cb.at[k, way, x_far, c], dst, x1_s.at[way, k], x1_r.at[way, k], d_xl if way else d_xr)

    def x2_copy(k, way):
        src = cb.at[k, :, x_left if way else x_right, c]
        dst = (xl2 if way else xr2).at[k]
        return rdma(src, dst, x2_s.at[way, k], x2_r.at[way, k], d_xl if way else d_xr)

    def zz_copy(way, m, first):
        k = 2 * m if way else jnp.maximum(2 * m - 1, 0)
        src, dst = zs.at[k], (zl_buf if way else zr).at[m]
        if first:
            src, dst = src.at[way], dst.at[way]
        return rdma(src, dst, zz_s.at[way, m], zz_r.at[way, m], d_zl if way else d_zr)

    def zz_wait(way, m):
        @pl.when(m == 0)
        def _():
            zz_copy(way, m, True).wait_recv()

        @pl.when(m > 0)
        def _():
            zz_copy(way, m, False).wait_recv()

    def sum_step(t, carry):
        @pl.when(t < nz)
        def _():
            s = dest_of(t)
            cols = pl.ds(pl.multiple_of(s * wid, wid), wid)
            o = mm(hp[...], wd[:, cols])
            cb[t, 0] = o.astype(bf16).reshape(NX, NC, rows, wid)
            dx = mm_nt(gg[...], wg[cols, :]) + mm_nt(gu[...], wu[cols, :])
            cb[t, 1] = dx.astype(bf16).reshape(NX, NC, rows, wid)
            cs_copy(t).start()

        if ny > 1:

            @pl.when(t == 0)
            def _():
                y_term(y_far)
                for way in range(2):
                    y1_copy(way).start()

        @pl.when((t >= 1) & (t < nz + 1))
        def _():
            k = t - 1
            cs_copy(k).wait_recv()
            cb[k, :, :, c] = (cb[k, :, :, c].astype(f32) + sb[k].astype(f32)).astype(bf16)
            for way in range(2):
                x1_copy(k, way).start()

        if ny > 1:

            @pl.when(t == 1)
            def _():
                y_term(y_right)
                y_term(y_left)

        @pl.when((t >= 2) & (t < nz + 2))
        def _():
            k = t - 2
            for way in range(2):
                x1_copy(k, way).wait_recv()
                to = x_left if way else x_right
                came = (xl1 if way else xr1)[k]
                cb[k, way, to, c] = (cb[k, way, to, c].astype(f32) + came.astype(f32)).astype(bf16)
                x2_copy(k, way).start()

        if ny > 1:

            @pl.when(t == min(4, nz + 2))
            def _():
                for way in range(2):
                    y1_copy(way).wait_recv()
                    to = y_left if way else y_right
                    came = (yl1 if way else yr1)[...]
                    wt[to, way] = (wt[to, way].astype(f32) + came.astype(f32)).astype(bf16)
                    y2_copy(way).start()
                y_term(y)

        @pl.when(t >= 3)
        def _():
            k = t - 3
            for way in range(2):
                x2_copy(k, way).wait_recv()
            got = cb[k, :, x, c].astype(f32) + xr2[k].astype(f32) + xl2[k].astype(f32)
            odd = lax.rem(k, 2)

            @pl.when(k == 0)
            def _():
                zs[0] = got.astype(bf16)
                for way in range(2):
                    zz_copy(way, 0, True).start()

            @pl.when((odd == 1) & (k < nz - 1))
            def _():
                m = (k + 1) // 2
                zz_wait(0, m - 1)
                zs[k] = (got + zr[m - 1].astype(f32)).astype(bf16)
                zz_copy(0, m, False).start()

            @pl.when((odd == 0) & (k > 0))
            def _():
                m = k // 2
                zz_wait(1, m - 1)
                zs[k] = (got + zl_buf[m - 1].astype(f32)).astype(bf16)
                zz_copy(1, m, False).start()

            @pl.when(k == nz - 1)
            def _():
                for way in range(2):
                    zz_copy(way, half - 1, half == 1).wait_recv()
                both = zr[half - 1].astype(f32) + zl_buf[half - 1].astype(f32)
                zs[k] = (got + both).astype(bf16)

        return carry

    lax.fori_loop(0, nz + 3, sum_step, 0)

    for a in range(2):
        final = zs[nz - 1, a]
        stacked = jnp.concatenate(
            [final[:, q * LANES : (q + 1) * LANES] for q in range(q_n)], axis=0
        )
        fp[:, a * packed : (a + 1) * packed, :] = (
            mm(permt[...], stacked).astype(bf16).reshape(nh, packed, LANES)
        )
    f_out = [
        rdma(fp.at[lax.rem(h + k + 1, nh)], hb2.at[k], f_s.at[k], f_r.at[k], dev)
        for k, dev in enumerate(d_h)
    ]
    for cp in f_out:
        cp.start()

    if ny > 1:
        for way in range(2):
            y2_copy(way).wait_recv()
        for k in range(2):
            total = wt[y, k].astype(f32) + yr2[k].astype(f32) + yl2[k].astype(f32)
            gd[:, k * wid : (k + 1) * wid] = total
    else:
        y_term(y)
        for k in range(2):
            gd[:, k * wid : (k + 1) * wid] = wt[y, k].astype(f32)

    for cp in f_out:
        cp.wait_recv()
    total = fp[h].astype(f32)
    for k in range(nh - 1):
        total = total + hb2[k].astype(f32)
    out[...] = total.astype(bf16)

    for cp in (*h_out, *f_out):
        cp.wait_send()
    for k in range(3):
        p_copy(k).wait_send()
    p_sib().wait_send()
    if ny > 1:
        for way in range(2):
            y1_copy(way).wait_send()
            y2_copy(way).wait_send()

    def z_drain(d, carry):
        for way in range(2):
            z_copy(way, d, False).wait_send()
        return carry

    def zz_drain(m, carry):
        for way in range(2):
            zz_copy(way, m, False).wait_send()
        return carry

    lax.fori_loop(0, half - 1, z_drain, 0)
    lax.fori_loop(1, half, zz_drain, 0)
    for way in range(2):
        z_copy(way, half - 1, True).wait_send()
        zz_copy(way, 0, True).wait_send()

    def drain(t, carry):
        for way in range(2):
            xa_copy(t, way).wait_send()
            xb_copy(t, way).wait_send()
            x1_copy(t, way).wait_send()
            x2_copy(t, way).wait_send()
        sib_copy(t).wait_send()
        cs_copy(t).wait_send()
        return carry

    lax.fori_loop(0, nz, drain, 0)


def permutations(nh, tok, q_n):
    rows, packed = nh * tok, q_n * tok
    perm = np.zeros((q_n * rows, nh * packed), np.float32)
    permp = np.zeros((rows, nh * P_ROWS), np.float32)
    for h in range(nh):
        for i in range(tok):
            permp[h * tok + i, h * P_ROWS + i] = 1
            for q in range(q_n):
                perm[q * rows + h * tok + i, h * packed + q * tok + i] = 1
    return tuple(jnp.asarray(a, bf16) for a in (perm, perm.T, permp))


def fused(blk, wg, wu, wd, ny, nh, nz, tok):
    width, hid = wg.shape
    wid = width // nz
    q_n = wid // LANES
    rows = nh * tok
    every = NX * NC * rows
    half = nz // 2
    perms = permutations(nh, tok, q_n)
    vmem, dma = pltpu.VMEM, pltpu.SemaphoreType.DMA
    n_blk = 2 * q_n * tok
    scratch = [
        vmem((nh, n_blk + P_ROWS, LANES), bf16),
        vmem((NX, NC, rows, LANES), bf16),
        vmem((nz, 2, NX, NC, rows, wid), bf16),
        vmem((width, hid), bf16),
        vmem((width, hid), bf16),
        vmem((hid, width), bf16),
        vmem((every, hid), f32),
        vmem((every, hid), f32),
        vmem((every, hid), f32),
        vmem((every, LANES), f32),
        vmem((every, hid), bf16),
        vmem((every, hid), bf16),
        vmem((every, hid), bf16),
        vmem((nz, 2, NX, NC, rows, wid), bf16),
        vmem((nz, 2, NX, rows, wid), bf16),
        vmem((nz, rows, wid), bf16),
        vmem((nz, rows, wid), bf16),
        vmem((nz, 2, rows, wid), bf16),
        vmem((nz, 2, rows, wid), bf16),
        vmem((nz, 2, rows, wid), bf16),
        vmem((half, 2, rows, wid), bf16),
        vmem((half, 2, rows, wid), bf16),
        vmem((nz // 2, 2, hid, wid), bf16),
        vmem((hid, wid), bf16),
        vmem((hid, wid), bf16),
        vmem((2, hid, wid), bf16),
        vmem((2, hid, wid), bf16),
        vmem((nh, n_blk, LANES), bf16),
        vmem((max(nh - 1, 1), n_blk, LANES), bf16),
        dma((3,)),
        dma((3,)),
        dma((3,)),
        dma((4,)),
        dma((4,)),
        dma((2, half)),
        dma((2, half)),
        dma((2, nz)),
        dma((2, nz)),
        dma((2, nz)),
        dma((2, nz)),
        dma((nz,)),
        dma((nz,)),
        dma((nz,)),
        dma((nz,)),
        dma((2, nz)),
        dma((2, nz)),
        dma((2, nz)),
        dma((2, nz)),
        dma((2, half)),
        dma((2, half)),
        dma((4,)),
        dma((4,)),
        dma((3,)),
        dma((3,)),
    ]
    in_vmem, anywhere = pl.BlockSpec(memory_space=pltpu.VMEM), pl.BlockSpec(memory_space=pl.ANY)
    return pl.pallas_call(
        functools.partial(kernel, ny, nh, nz, tok, wid),
        out_shape=(
            jax.ShapeDtypeStruct((n_blk, LANES), bf16),
            jax.ShapeDtypeStruct((hid, 2 * wid), f32),
        ),
        in_specs=[in_vmem] * 4 + [anywhere] * 3,
        out_specs=(in_vmem, in_vmem),
        scratch_shapes=scratch,
        compiler_params=pltpu.CompilerParams(
            collective_id=0, has_side_effects=True, vmem_limit_bytes=VMEM_BYTES
        ),
        cost_estimate=pl.CostEstimate(
            flops=14 * every * width * hid, bytes_accessed=6 * width * hid, transcendentals=every * hid
        ),
    )(blk, *perms, wg, wu, wd)


def on_device(tokens, grad_out, route_ids, route_probs, w_gate, w_up, w_down):
    tok, wid = tokens.shape
    q_n = wid // LANES
    ny, nz = lax.axis_size("dp"), lax.axis_size("tensor")
    nh = lax.axis_size("expert") // (NX * NC)

    def pack(a):
        return a.reshape(tok, q_n, LANES).transpose(1, 0, 2).reshape(q_n * tok, LANES)

    def unpack(a):
        return a.reshape(q_n, tok, LANES).transpose(1, 0, 2).reshape(tok, wid)

    named = route_ids[:, :, None] == jnp.arange(EXPERTS, dtype=jnp.int32)
    dense = jnp.sum(jnp.where(named, route_probs[:, :, None], 0.0), axis=1)
    high = lax.reduce_precision(dense, 8, 7)
    middle = lax.reduce_precision(dense - high, 8, 7)
    pieces = jnp.concatenate([high, middle, dense - high - middle], axis=1).astype(bf16)
    pieces = jnp.pad(pieces, ((0, P_ROWS - tok), (0, LANES - 3 * EXPERTS)))
    blk = jnp.concatenate([pack(tokens), pack(grad_out), pieces], axis=0)
    both, grad_down = fused(blk, w_gate[0], w_up[0], w_down[0], ny, nh, nz, tok)
    mixed, grad_tokens = unpack(both[: q_n * tok]), unpack(both[q_n * tok :])
    return (mixed, grad_tokens, grad_down[None])


def solution(mesh):
    return jax.shard_map(
        on_device,
        mesh=mesh,
        in_specs=(
            P(("dp", "expert"), "tensor"),
            P(("dp", "expert"), "tensor"),
            P(("dp", "expert"), None),
            P(("dp", "expert"), None),
            P("expert", None, "tensor"),
            P("expert", None, "tensor"),
            P("expert", "tensor", None),
        ),
        out_specs=(
            P(("dp", "expert"), "tensor"),
            P(("dp", "expert"), "tensor"),
            P("expert", "tensor", "dp"),
        ),
        check_vma=False,
    )
```

time: 2370 us -> 152 us (0.06)
  the two profiles are of different devices: /device:TPU:10 before, /device:TPU:24 now
where the time goes in v2:
time: 152 us; the launch traced here: 151 us
  Pallas kernels  136 us (89%)
  local copies, waits for them, and re-layouts  13.5 us (9%)
    pallas_call x1, Pallas kernels, fused(): pl.pallas_call(functools.partial(kernel, ny, nh, nz, tok, wid), out_shape...  136 us
    unnamed x11, local copies, waits for them, and re-layouts  11.3 us

profile of v2, /device:TPU:24, one launch (start us, length us, event | category | flops | bytes accessed | tf_op | source)
XLA Modules:
  0.0 150.8 jit_solution(5990016273139582850)
XLA Ops:
  0.6 0.8 copy.37
  1.4 0.8 copy.38
  2.2 0.1 select_reduce_fusion
  2.3 0.1 fusion.9
  2.4 0.7 reshape.32
  3.1 0.7 reshape.34
  3.9 0.6 pad_maximum_fusion.blk
  4.5 0.0 copy-start
  4.5 4.0 %copy.39 = bf16[1,4096,192]{2,1,0:T(8,128)(2,1)} copy(bf16[1,4096,192]{1,2,0:T(8,128)(2,1)} %param.14) | data formatting | bytes 3145728 | tf_op args[4]
  8.5 0.0 copy-done
  8.5 2.4 %copy.40 = bf16[1,4096,192]{2,1,0:T(8,128)(2,1)} copy(bf16[1,4096,192]{1,2,0:T(8,128)(2,1)S(1)} %copy-done) | data formatting | bytes 3145728 | tf_op args[5]
  10.9 135.7 %shard_map.121 = (bf16[96,128]{1,0:T(8,128)(2,1)}, f32[192,1024]{1,0:T(8,128)}) custom-call(bf16[112,128]{1,0:T(8,128)(2,1)} %pad_maximum_fusion.blk, bf16[192,192]{1,0:T(8,128)(2,1)} %constant.9.clone.perm.permt, bf16[192,192]{1,0:T(8,128)(2,1)} %constant.9.clone.perm.permt, bf16[48,64]{1,0:T(8,128)(2,1)} %constant.10.clone.permp, ...), custom_call_target="tpu_custom_call" | custom-call | flops 4227858432 | bytes 4718592 | tf_op jit(solution)/shard_map/pallas_call | solution.py:533
  146.7 0.7 fusion.10
  147.4 0.6 copy.44
  148.1 0.6 copy.43
  148.7 2.1 %copy.50 = f32[1,192,1024]{2,1,0:T(8,128)} copy(f32[1,192,1024]{2,1,0:T(8,128)} %bitcast.20) | data formatting | bytes 1572864
  (11 shorter events, 0.1 us)
Async XLA Ops:
  4.5 4.0 %copy-start = (bf16[1,4096,192]{1,2,0:T(8,128)(2,1)S(1)}, bf16[1,4096,192]{1,2,0:T(8,128)(2,1)}, u32[]{:S(2)}) copy-start(bf16[1,4096,192]{1,2,0:T(8,128)(2,1)} %param.15) | copy-start | bytes 4718596

commit v3 on v2

--- a/solution.py
+++ b/solution.py
@@ -9,6 +9,7 @@
 from jax.sharding import PartitionSpec as P
 
 EXPERTS = 32
+TOPK = 8
 AMAX_TARGET = 4.0
 EPS_SCALE = 1e-05
 LANES = 128
@@ -33,9 +34,9 @@
 
 def kernel(
     ny, nh, nz, tok, wid,
-    blk, perm, permt, permp, wg_h, wu_h, wd_h,
-    out, gd,
-    hbuf, pb, xb, wg, wu, wd, gate_acc, up_acc, gh_acc, amax, hp, gg, gu,
+    tok_in, go_in, ids_in, probs_in, perm, permt, permp, spread_p, gather_p, wg_h, wu_h, wd_h,
+    out_m, out_g, gd,
+    blk, pad_in, hbuf, pb, xb, wg, wu, wd, gate_acc, up_acc, gh_acc, amax, hp, gg, gu,
     cb, sb, xr1, xl1, xr2, xl2, zs, zr, zl_buf, wt, yr1, yl1, yr2, yl2, fp, hb2,
     w_sem, h_s, h_r, p_s, p_r, z_s, z_r, xa_s, xa_r, xb_s, xb_r, sib_s, sib_r,
     cs_s, cs_r, x1_s, x1_r, x2_s, x2_r, zz_s, zz_r, y_s, y_r, f_s, f_r,
@@ -83,13 +84,21 @@
     barrier = pltpu.get_barrier_semaphore()
     for dev in partners:
         pl.semaphore_signal(barrier, inc=1, device_id=dev, device_id_type=MESH)
-    pl.semaphore_wait(barrier, len(partners))
-
-    h_out = [
-        rdma(blk, hbuf.at[h], h_s.at[k], h_r.at[k], dev) for k, dev in enumerate(d_h)
-    ]
-    for cp in h_out:
-        cp.start()
+
+    pad_in[...] = jnp.zeros_like(pad_in)
+    for a, ref in enumerate((tok_in, go_in)):
+        pad_in[:tok, :] = ref[...]
+        tall = jnp.concatenate([pad_in[:, q * LANES : (q + 1) * LANES] for q in range(q_n)], axis=0)
+        blk[a * packed : (a + 1) * packed, :] = mm(gather_p[...], tall).astype(bf16)
+    expert = lax.broadcasted_iota(jnp.int32, (EXPERTS, LANES), 0)
+    dense = jnp.zeros((EXPERTS, LANES), f32)
+    for k in range(TOPK):
+        dense = dense + jnp.where(expert == ids_in[k : k + 1, :], probs_in[k : k + 1, :], 0.0)
+    high = dense.astype(bf16).astype(f32)
+    middle = (dense - high).astype(bf16).astype(f32)
+    tall = jnp.concatenate([high, middle, dense - high - middle, jnp.zeros_like(dense)], axis=0)
+    blk[2 * packed :, :] = tall.T[:P_ROWS].astype(bf16)
+
     hbuf[pl.ds(h, 1)] = blk[...][None]
     gate_acc[...] = jnp.zeros_like(gate_acc)
     up_acc[...] = jnp.zeros_like(up_acc)
@@ -97,6 +106,13 @@
     amax[...] = jnp.zeros_like(amax)
     zr[0, 1] = jnp.zeros_like(zr[0, 1])
     zl_buf[0, 0] = jnp.zeros_like(zl_buf[0, 0])
+    pl.semaphore_wait(barrier, len(partners))
+
+    h_out = [
+        rdma(blk, hbuf.at[h], h_s.at[k], h_r.at[k], dev) for k, dev in enumerate(d_h)
+    ]
+    for cp in h_out:
+        cp.start()
     for cp in h_out:
         cp.wait_recv()
     for a in range(2):
@@ -208,8 +224,8 @@
             s = at_step(t - 3)
             cols = pl.ds(pl.multiple_of(s * wid, wid), wid)
             x_rows = xb[s, 0].reshape(every, wid)
-            gate_acc[...] += mm(x_rows, wg[cols, :])
-            up_acc[...] += mm(x_rows, wu[cols, :])
+            gate_acc[...] += mm_nt(x_rows, wg[:, cols])
+            up_acc[...] += mm_nt(x_rows, wu[:, cols])
             gh_acc[...] += mm_nt(xb[s, 1].reshape(every, wid), wd[:, cols])
             size = jnp.abs(x_rows.astype(f32))
             top = amax[...]
@@ -291,7 +307,7 @@
             cols = pl.ds(pl.multiple_of(s * wid, wid), wid)
             o = mm(hp[...], wd[:, cols])
             cb[t, 0] = o.astype(bf16).reshape(NX, NC, rows, wid)
-            dx = mm_nt(gg[...], wg[cols, :]) + mm_nt(gu[...], wu[cols, :])
+            dx = mm(gg[...], wg[:, cols]) + mm(gu[...], wu[:, cols])
             cb[t, 1] = dx.astype(bf16).reshape(NX, NC, rows, wid)
             cs_copy(t).start()
 
@@ -410,7 +426,11 @@
     total = fp[h].astype(f32)
     for k in range(nh - 1):
         total = total + hb2[k].astype(f32)
-    out[...] = total.astype(bf16)
+    total = total.astype(bf16)
+    for a, ref in enumerate((out_m, out_g)):
+        tall = mm(spread_p[...], total[a * packed : (a + 1) * packed]).astype(bf16)
+        for q in range(q_n):
+            ref[:, q * LANES : (q + 1) * LANES] = tall[q * P_ROWS : q * P_ROWS + tok]
 
     for cp in (*h_out, *f_out):
         cp.wait_send()
@@ -455,16 +475,20 @@
     rows, packed = nh * tok, q_n * tok
     perm = np.zeros((q_n * rows, nh * packed), np.float32)
     permp = np.zeros((rows, nh * P_ROWS), np.float32)
+    spread = np.zeros((q_n * P_ROWS, packed), np.float32)
+    for q in range(q_n):
+        for i in range(tok):
+            spread[q * P_ROWS + i, q * tok + i] = 1
     for h in range(nh):
         for i in range(tok):
             permp[h * tok + i, h * P_ROWS + i] = 1
             for q in range(q_n):
                 perm[q * rows + h * tok + i, h * packed + q * tok + i] = 1
-    return tuple(jnp.asarray(a, bf16) for a in (perm, perm.T, permp))
-
-
-def fused(blk, wg, wu, wd, ny, nh, nz, tok):
-    width, hid = wg.shape
+    return tuple(jnp.asarray(a, bf16) for a in (perm, perm.T, permp, spread, spread.T))
+
+
+def fused(tokens, grad_out, ids, probs, wg, wu, wd, ny, nh, nz, tok):
+    hid, width = wg.shape
     wid = width // nz
     q_n = wid // LANES
     rows = nh * tok
@@ -474,11 +498,13 @@
     vmem, dma = pltpu.VMEM, pltpu.SemaphoreType.DMA
     n_blk = 2 * q_n * tok
     scratch = [
+        vmem((n_blk + P_ROWS, LANES), bf16),
+        vmem((P_ROWS, wid), bf16),
         vmem((nh, n_blk + P_ROWS, LANES), bf16),
         vmem((NX, NC, rows, LANES), bf16),
         vmem((nz, 2, NX, NC, rows, wid), bf16),
-        vmem((width, hid), bf16),
-        vmem((width, hid), bf16),
+        vmem((hid, width), bf16),
+        vmem((hid, width), bf16),
         vmem((hid, width), bf16),
         vmem((every, hid), f32),
         vmem((every, hid), f32),
@@ -533,11 +559,12 @@
     return pl.pallas_call(
         functools.partial(kernel, ny, nh, nz, tok, wid),
         out_shape=(
-            jax.ShapeDtypeStruct((n_blk, LANES), bf16),
+            jax.ShapeDtypeStruct((tok, wid), bf16),
+            jax.ShapeDtypeStruct((tok, wid), bf16),
             jax.ShapeDtypeStruct((hid, 2 * wid), f32),
         ),
-        in_specs=[in_vmem] * 4 + [anywhere] * 3,
-        out_specs=(in_vmem, in_vmem),
+        in_specs=[in_vmem] * 9 + [anywhere] * 3,
+        out_specs=(in_vmem, in_vmem, in_vmem),
         scratch_shapes=scratch,
         compiler_params=pltpu.CompilerParams(
             collective_id=0, has_side_effects=True, vmem_limit_bytes=VMEM_BYTES
@@ -545,30 +572,17 @@
         cost_estimate=pl.CostEstimate(
             flops=14 * every * width * hid, bytes_accessed=6 * width * hid, transcendentals=every * hid
         ),
-    )(blk, *perms, wg, wu, wd)
+    )(tokens, grad_out, ids, probs, *perms, wg, wu, wd)
 
 
 def on_device(tokens, grad_out, route_ids, route_probs, w_gate, w_up, w_down):
     tok, wid = tokens.shape
-    q_n = wid // LANES
     ny, nz = lax.axis_size("dp"), lax.axis_size("tensor")
     nh = lax.axis_size("expert") // (NX * NC)
-
-    def pack(a):
-        return a.reshape(tok, q_n, LANES).transpose(1, 0, 2).reshape(q_n * tok, LANES)
-
-    def unpack(a):
-        return a.reshape(q_n, tok, LANES).transpose(1, 0, 2).reshape(tok, wid)
-
-    named = route_ids[:, :, None] == jnp.arange(EXPERTS, dtype=jnp.int32)
-    dense = jnp.sum(jnp.where(named, route_probs[:, :, None], 0.0), axis=1)
-    high = lax.reduce_precision(dense, 8, 7)
-    middle = lax.reduce_precision(dense - high, 8, 7)
-    pieces = jnp.concatenate([high, middle, dense - high - middle], axis=1).astype(bf16)
-    pieces = jnp.pad(pieces, ((0, P_ROWS - tok), (0, LANES - 3 * EXPERTS)))
-    blk = jnp.concatenate([pack(tokens), pack(grad_out), pieces], axis=0)
-    both, grad_down = fused(blk, w_gate[0], w_up[0], w_down[0], ny, nh, nz, tok)
-    mixed, grad_tokens = unpack(both[: q_n * tok]), unpack(both[q_n * tok :])
+    ids, probs = (jnp.pad(a.T, ((0, 0), (0, LANES - tok))) for a in (route_ids, route_probs))
+    mixed, grad_tokens, grad_down = fused(
+        tokens, grad_out, ids, probs, w_gate[0].T, w_up[0].T, w_down[0], ny, nh, nz, tok
+    )
     return (mixed, grad_tokens, grad_down[None])
 
 

time: 152 us -> 145 us (0.954)
  local copies, waits for them, and re-layouts: 13.5 us -> 7.3 us
    unnamed x11 -> x3, local copies, waits for them, and re-layouts: 11.3 us -> 4.73 us
    pad x0 -> x2, local copies, waits for them, and re-layouts: none -> 2.57 us  [on_device(): jnp.pad(a.T, ((0, 0), (0, LANES - tok)))]
    reshape x8 -> x0, local copies, waits for them, and re-layouts: 1.52 us -> none  [the longest x6 1.5 us: pack(): a.reshape(tok, q_n, LANES).transpose(1, 0, 2).reshape(q_n * tok, LANES)]
where the time goes in v3:
time: 145 us; the launch traced here: 144 us
  Pallas kernels  136 us (94%)
  local copies, waits for them, and re-layouts  7.3 us (5%)
    pallas_call x1, Pallas kernels, fused(): pl.pallas_call(functools.partial(kernel, ny, nh, nz, tok, wid), out_shape...  136 us
    unnamed x3, local copies, waits for them, and re-layouts  4.73 us

profile of v3, /device:TPU:24, one launch (start us, length us, event | category | flops | bytes accessed | tf_op | source)
XLA Modules:
  0.0 143.9 jit_solution(11289467977494649967)
XLA Ops:
  0.6 1.3 pad.8.ids_in
  1.9 1.3 pad.9.probs_in
  3.2 135.9 %shard_map.139 = (bf16[12,512]{1,0:T(8,128)(2,1)}, bf16[12,512]{1,0:T(8,128)(2,1)}, f32[192,1024]{1,0:T(8,128)}) custom-call(bf16[12,512]{1,0:T(8,128)(2,1)} %tok_in.1, bf16[12,512]{1,0:T(8,128)(2,1)} %go_in.1, s32[8,128]{1,0:T(8,128)} %pad.8.ids_in, f32[8,128]{1,0:T(8,128)} %pad.9.probs_in, bf16[192,192]{1,0:T(8,128)(2,1)} %constant.10.clone.perm.permt, ...), custom_call_target="tpu_custom_call" | custom-call | flops 4227858432 | bytes 4718592 | tf_op jit(solution)/shard_map/pallas_call | solution.py:559
  139.1 1.3 copy.18
  140.5 1.3 copy.19
  141.8 2.1 %copy.20 = f32[1,192,1024]{2,1,0:T(8,128)} copy(f32[1,192,1024]{2,1,0:T(8,128)} %bitcast.10) | data formatting | bytes 1572864

commit v4 on v3

v4 whole, which is shorter than its diff:
```python
import functools

import jax
import jax.numpy as jnp
import numpy as np
from jax import lax
from jax.experimental import pallas as pl
from jax.experimental.pallas import tpu as pltpu
from jax.sharding import PartitionSpec as P

EXPERTS = 32
TOPK = 8
AMAX_TARGET = 4.0
EPS_SCALE = 1e-05
LANES = 128
NX, NC = 4, 2
SLOT = 16
bf16, f32 = jnp.bfloat16, jnp.float32
MESH = pl.DeviceIdType.MESH
VMEM_BYTES = 56 * 1024 * 1024


def mm(a, b):
    return jnp.dot(a, b, preferred_element_type=f32)


def mm_nt(a, b):
    return lax.dot_general(a, b, (((1,), (1,)), ((), ())), preferred_element_type=f32)


def mm_tn(a, b):
    return lax.dot_general(a, b, (((0,), (0,)), ((), ())), preferred_element_type=f32)


def kernel(
    ny, nh, nz, tok, wid,
    tok_in, go_in, ids_in, probs_in, grow_one, shrink_one, wg_h, wu_h, wd_h,
    out_m, out_g, gd,
    pad_in, pb, xb, g4, wg, wu, wd, gate_acc, up_acc, gh_acc, amax, hp, gg, gu,
    cb, sb, xr1, xl1, xr2, xl2, zs, zr, zl_buf, wt, yr1, yl1, yr2, yl2, far,
    w_sem, h_s, h_r, hp_s, hp_r, p_s, p_r, z_s, z_r, xa_s, xa_r, xb_s, xb_r, sib_s, sib_r,
    cs_s, cs_r, x1_s, x1_r, x2_s, x2_r, zz_s, zz_r, y_s, y_r, f_s, f_r,
):
    half = nz // 2
    items = nh * nz
    main = wid - LANES
    groups = main // LANES
    rows = nh * SLOT
    every = NX * NC * rows
    y, e, z = lax.axis_index("dp"), lax.axis_index("expert"), lax.axis_index("tensor")
    c = lax.rem(e, NC)
    x = lax.rem(e // NC, NX)
    h = e // (NC * NX)
    place = h * nz + z

    def eid(h_, x_, c_):
        return (h_ * NX + x_) * NC + c_

    x_right, x_left, x_far = (lax.rem(x + k, NX) for k in (1, 3, 2))
    d_xr, d_xl, d_xf = ((y, eid(h, k, c), z) for k in (x_right, x_left, x_far))
    d_sib = (y, eid(h, x, 1 - c), z)
    d_zr = (y, eid(lax.rem(h + (z + 1) // nz, nh), x, c), lax.rem(z + 1, nz))
    d_zl = (
        y,
        eid(lax.rem(h + nh - 1 + (z + nz - 1) // nz, nh), x, c),
        lax.rem(z + nz - 1, nz),
    )
    jumps = [(0, 1, 3, 2)[r] % nh for r in range(nh)]
    d_h = [(y, eid(lax.rem(h + j, nh), x, c), z) for j in jumps]
    d_yr, d_yl = (lax.rem(y + 1, ny), e, z), (lax.rem(y + ny - 1, ny), e, z)

    def jump(r):
        return jnp.where(r < 2, r, 5 - r)

    def slot(p):
        return pl.ds(pl.multiple_of((p // nz) * SLOT, SLOT), SLOT)

    def rdma(src, dst, s, r, dev):
        return pltpu.make_async_remote_copy(
            src_ref=src, dst_ref=dst, send_sem=s, recv_sem=r, device_id=dev, device_id_type=MESH
        )

    loads = [
        pltpu.make_async_copy(a, b, w_sem.at[i])
        for i, (a, b) in enumerate(((wg_h, wg), (wu_h, wu), (wd_h, wd)))
    ]
    for load in loads:
        load.start()

    partners = [d_xr, d_xl, d_xf, d_sib, d_zr, d_zl, *d_h[1:]]
    if ny > 1:
        partners += [d_yr, d_yl]
    barrier = pltpu.get_barrier_semaphore()
    for dev in partners:
        pl.semaphore_signal(barrier, inc=1, device_id=dev, device_id_type=MESH)

    own = slot(place)
    sub = lax.broadcasted_iota(jnp.int32, (every // SLOT, 8, LANES), 1)
    pad_in[...] = jnp.zeros_like(pad_in)
    for a, ref in enumerate((tok_in, go_in)):
        pad_in[:tok, :] = ref[...]
        for g in range(groups):
            lanes = slice(g * LANES, (g + 1) * LANES)
            moved = mm(shrink_one[g], pad_in[:, main:])
            xb[z, a, x, c, own, lanes] = (pad_in[:, lanes].astype(f32) + moved).astype(bf16)
    expert = lax.broadcasted_iota(jnp.int32, (EXPERTS, LANES), 0)
    dense = jnp.zeros((EXPERTS, LANES), f32)
    for k in range(TOPK):
        dense = dense + jnp.where(expert == ids_in[k : k + 1, :], probs_in[k : k + 1, :], 0.0)
    high = dense.astype(bf16).astype(f32)
    middle = (dense - high).astype(bf16).astype(f32)
    tall = jnp.concatenate([high, middle, dense - high - middle, jnp.zeros_like(dense)], axis=0)
    pb[x, c, own] = tall.T[:SLOT].astype(bf16)
    gate_acc[...] = jnp.zeros_like(gate_acc)
    up_acc[...] = jnp.zeros_like(up_acc)
    gh_acc[...] = jnp.zeros_like(gh_acc)
    amax[...] = jnp.zeros_like(amax)
    zr[0, 1] = jnp.zeros_like(zr[0, 1])
    zl_buf[0, 0] = jnp.zeros_like(zl_buf[0, 0])
    pl.semaphore_wait(barrier, len(partners))

    back = [jumps.index((nh - j) % nh) for j in jumps]
    h_out = [
        rdma(xb.at[z, :, x, c, own], xb.at[z, :, x, c, own], h_s.at[r], h_r.at[back[r]], d_h[r])
        for r in range(1, nh)
    ]
    hp_out = [
        rdma(pb.at[x, c, own], pb.at[x, c, own], hp_s.at[r], hp_r.at[r], d_h[r])
        for r in range(1, nh)
    ]
    for cp, cp_p in zip(h_out, hp_out):
        cp.start()
        cp_p.start()

    others = max(nh - 1, 1)

    def turn(u):
        w = jnp.maximum(u - nz, 0)
        first = u < nz
        return jnp.where(first, 0, 1 + lax.rem(w, others)), jnp.where(first, u, w // others)

    def source(u):
        r, t = turn(u)
        d = (t + 1) // 2
        return lax.rem(place + d * (1 - 2 * lax.rem(t, 2)) + nz * jump(r) + items, items)

    def z_copy(way, r, d):
        p = lax.rem(place + (d if way else -d) + nz * jump(r) + items, items)
        ref = xb.at[lax.rem(p, nz), :, x, c, slot(p)]
        i = r * half + d
        return rdma(ref, ref, z_s.at[way, i], z_r.at[way, i], d_zl if way else d_zr)

    def xa_copy(u, way):
        p = source(u)
        ref = xb.at[lax.rem(p, nz), :, x, c, slot(p)]
        return rdma(ref, ref, xa_s.at[way, u], xa_r.at[way, u], d_xl if way else d_xr)

    def xb_copy(u, way):
        p = source(u)
        ref = xb.at[lax.rem(p, nz), :, x_right if way else x_left, c, slot(p)]
        return rdma(ref, ref, xb_s.at[u], xb_r.at[u], d_xl if way else d_xr)

    def sib_copy(u):
        p = source(u)
        ref = xb.at[lax.rem(p, nz), :, :, c, slot(p)]
        return rdma(ref, ref, sib_s.at[u], sib_r.at[u], d_sib)

    def p_copy(k):
        ref = pb.at[x, c]
        return rdma(ref, ref, p_s.at[k], p_r.at[k], (d_xr, d_xl, d_xf)[k])

    def p_sib():
        ref = pb.at[:, c]
        return rdma(ref, ref, p_s.at[3], p_r.at[3], d_sib)

    p_at = items - 8 if items > 8 else 0
    lag_a, lag_b, lag_c = 4, 7, 9

    def gather_step(v, carry):
        @pl.when(v < items)
        def _():
            r, t = turn(v)
            d = (t + 1) // 2
            odd = lax.rem(t, 2)
            for k in range(1, nh):

                @pl.when(v == nz + k - 1)
                def _():
                    h_out[back[k] - 1].wait_recv()

            @pl.when((t > 0) & (odd == 1))
            def _():
                z_copy(0, r, d - 1).wait_recv()

            @pl.when((t > 0) & (odd == 0))
            def _():
                z_copy(1, r, d - 1).wait_recv()

            @pl.when(((t == 0) | (odd == 1)) & (d < half))
            def _():
                z_copy(0, r, d).start()

            @pl.when((odd == 0) & (d < half - 1))
            def _():
                z_copy(1, r, d).start()

            for way in range(2):
                xa_copy(v, way).start()

            @pl.when(v == p_at)
            def _():
                for cp in hp_out:
                    cp.wait_recv()
                for k in range(3):
                    p_copy(k).start()

        @pl.when((v >= lag_a) & (v < items + lag_a))
        def _():
            u = v - lag_a
            for way in range(2):
                xa_copy(u, way).wait_recv()

                @pl.when(lax.rem(u, 2) == way)
                def _():
                    xb_copy(u, way).start()

        @pl.when((v >= lag_b) & (v < items + lag_b))
        def _():
            u = v - lag_b
            xb_copy(u, 0).wait_recv()
            sib_copy(u).start()

            @pl.when(u == p_at)
            def _():
                for k in range(3):
                    p_copy(k).wait_recv()
                p_sib().start()

        @pl.when(v == 3)
        def _():
            for load in loads:
                load.wait()

        @pl.when(v >= lag_c)
        def _():
            sib_copy(v - lag_c).wait_recv()

        @pl.when((v - lag_c >= (nz if nh > 1 else 0)) & (turn(jnp.maximum(v - lag_c, 0))[0] == nh - 1))
        def _():
            s = lax.rem(source(v - lag_c), nz)
            cols = pl.ds(pl.multiple_of(s * wid, wid), wid)

            def whole(a):
                part = xb[s, a].reshape(every, main)
                end = part.astype(f32).reshape(every // SLOT, SLOT, main)[:, 8:]
                first, second, third = (end[..., g * LANES : (g + 1) * LANES] for g in range(groups))
                upper = jnp.where(sub < 4, pltpu.roll(first, 4, 1), second)
                lower = jnp.where(sub < 4, pltpu.roll(third, 4, 1), 0.0)
                rest = jnp.concatenate([upper, lower], axis=1).reshape(every, LANES)
                return part, rest.astype(bf16)

            x_part, x_rest = whole(0)
            x_rows = jnp.concatenate([x_part, x_rest], axis=1)
            gate_acc[...] += mm_nt(x_rows, wg[:, cols])
            up_acc[...] += mm_nt(x_rows, wu[:, cols])
            g_part, g_rest = whole(1)
            g4[s] = g_rest
            gh_acc[...] += mm_nt(jnp.concatenate([g_part, g_rest], axis=1), wd[:, cols])
            size = jnp.abs(x_rows.astype(f32))
            top = amax[...]
            for q in range(groups + 1):
                top = jnp.maximum(top, size[:, q * LANES : (q + 1) * LANES])
            amax[...] = top

        return carry

    lax.fori_loop(0, items + lag_c, gather_step, 0)

    p_sib().wait_recv()
    lane = lax.broadcasted_iota(jnp.int32, (every, LANES), 1)
    mine = (lane == e) | (lane == e + EXPERTS) | (lane == e + 2 * EXPERTS)
    prob = jnp.sum(
        jnp.where(mine, pb[...].reshape(every, LANES).astype(f32), 0.0), axis=1, keepdims=True
    )
    factor = AMAX_TARGET / (jnp.max(amax[...], axis=1, keepdims=True) + EPS_SCALE)
    gate = gate_acc[...] * factor
    upval = up_acc[...] * factor
    sigma = jax.nn.sigmoid(gate)
    active = gate * sigma
    grad = gh_acc[...] * (prob * factor)
    hp[...] = (prob * active * upval).astype(bf16)
    gg[...] = (grad * upval * sigma * (1.0 + gate * (1.0 - sigma))).astype(bf16)
    gu[...] = (grad * active).astype(bf16)

    def y_term(dest):
        for k in range(2):
            s = 2 * dest + k
            wt[dest, k, :, :main] = mm_tn(hp[...], xb[s, 1].reshape(every, main)).astype(bf16)
            wt[dest, k, :, main:] = mm_tn(hp[...], g4[s]).astype(bf16)

    y_far, y_right, y_left = (lax.rem(y + k, ny) for k in (2, 1, 3))

    def y1_copy(way):
        src, dst = wt.at[y_far, way], (yl1 if way else yr1)
        return rdma(src, dst, y_s.at[way], y_r.at[way], d_yl if way else d_yr)

    def y2_copy(way):
        src, dst = wt.at[y_left if way else y_right], (yl2 if way else yr2)
        return rdma(src, dst, y_s.at[2 + way], y_r.at[2 + way], d_yl if way else d_yr)

    def dest_of(k):
        odd = lax.rem(k, 2)
        off = jnp.where(odd == 1, half - (k + 1) // 2, k // 2 - half)
        return lax.rem(z + off + nz, nz)

    def cs_copy(k):
        return rdma(cb.at[k, :, :, 1 - c], sb.at[k], cs_s.at[k], cs_r.at[k], d_sib)

    def x1_copy(k, way):
        dst = (xl1 if way else xr1).at[k]
        return rdma(cb.at[k, way, x_far, c], dst, x1_s.at[way, k], x1_r.at[way, k], d_xl if way else d_xr)

    def x2_copy(k, way):
        src = cb.at[k, :, x_left if way else x_right, c]
        dst = (xl2 if way else xr2).at[k]
        return rdma(src, dst, x2_s.at[way, k], x2_r.at[way, k], d_xl if way else d_xr)

    def zz_copy(way, m, first):
        k = 2 * m if way else jnp.maximum(2 * m - 1, 0)
        src, dst = zs.at[k], (zl_buf if way else zr).at[m]
        if first:
            src, dst = src.at[way], dst.at[way]
        return rdma(src, dst, zz_s.at[way, m], zz_r.at[way, m], d_zl if way else d_zr)

    def zz_wait(way, m):
        @pl.when(m == 0)
        def _():
            zz_copy(way, m, True).wait_recv()

        @pl.when(m > 0)
        def _():
            zz_copy(way, m, False).wait_recv()

    def packed(value):
        last = value[:, main:].reshape(every // SLOT, SLOT, LANES)
        moved = (pltpu.roll(last[:, :8], 4, 1), last[:, :8], pltpu.roll(last[:, 8:], 4, 1))
        parts = []
        for g in range(groups):
            lanes = value[:, g * LANES : (g + 1) * LANES].reshape(every // SLOT, SLOT, LANES)
            lower = jnp.where(sub < 4, lanes[:, 8:], moved[g])
            parts.append(jnp.concatenate([lanes[:, :8], lower], axis=1).reshape(every, LANES).astype(bf16))
        return jnp.concatenate(parts, axis=1).reshape(NX, NC, rows, main)

    def sum_step(t, carry):
        @pl.when(t < nz)
        def _():
            s = dest_of(t)
            cols = pl.ds(pl.multiple_of(s * wid, wid), wid)
            cb[t, 0] = packed(mm(hp[...], wd[:, cols]))
            cb[t, 1] = packed(mm(gg[...], wg[:, cols]) + mm(gu[...], wu[:, cols]))
            cs_copy(t).start()

        if ny > 1:

            @pl.when(t == 0)
            def _():
                y_term(y_far)
                for way in range(2):
                    y1_copy(way).start()

        @pl.when((t >= 1) & (t < nz + 1))
        def _():
            k = t - 1
            cs_copy(k).wait_recv()
            cb[k, :, :, c] = (cb[k, :, :, c].astype(f32) + sb[k].astype(f32)).astype(bf16)
            for way in range(2):
                x1_copy(k, way).start()

        if ny > 1:

            @pl.when(t == 1)
            def _():
                y_term(y_right)
                y_term(y_left)

        @pl.when((t >= 2) & (t < nz + 2))
        def _():
            k = t - 2
            for way in range(2):
                x1_copy(k, way).wait_recv()
                to = x_left if way else x_right
                came = (xl1 if way else xr1)[k]
                cb[k, way, to, c] = (cb[k, way, to, c].astype(f32) + came.astype(f32)).astype(bf16)
                x2_copy(k, way).start()

        if ny > 1:

            @pl.when(t == min(4, nz + 2))
            def _():
                for way in range(2):
                    y1_copy(way).wait_recv()
                    to = y_left if way else y_right
                    came = (yl1 if way else yr1)[...]
                    wt[to, way] = (wt[to, way].astype(f32) + came.astype(f32)).astype(bf16)
                    y2_copy(way).start()
                y_term(y)

        @pl.when(t >= 3)
        def _():
            k = t - 3
            for way in range(2):
                x2_copy(k, way).wait_recv()
            got = cb[k, :, x, c].astype(f32) + xr2[k].astype(f32) + xl2[k].astype(f32)
            odd = lax.rem(k, 2)

            @pl.when(k == 0)
            def _():
                zs[0] = got.astype(bf16)
                for way in range(2):
                    zz_copy(way, 0, True).start()

            @pl.when((odd == 1) & (k < nz - 1))
            def _():
                m = (k + 1) // 2
                zz_wait(0, m - 1)
                zs[k] = (got + zr[m - 1].astype(f32)).astype(bf16)
                zz_copy(0, m, False).start()

            @pl.when((odd == 0) & (k > 0))
            def _():
                m = k // 2
                zz_wait(1, m - 1)
                zs[k] = (got + zl_buf[m - 1].astype(f32)).astype(bf16)
                zz_copy(1, m, False).start()

            @pl.when(k == nz - 1)
            def _():
                for way in range(2):
                    zz_copy(way, half - 1, half == 1).wait_recv()
                both = zr[half - 1].astype(f32) + zl_buf[half - 1].astype(f32)
                zs[k] = (got + both).astype(bf16)

        return carry

    lax.fori_loop(0, nz + 3, sum_step, 0)

    def f_copy(r):
        src = zs.at[nz - 1, :, slot(lax.rem(place + nz * jumps[r], items))]
        return rdma(src, far.at[r - 1], f_s.at[r], f_r.at[r], d_h[r])

    for r in range(1, nh):
        f_copy(r).start()

    if ny > 1:
        for way in range(2):
            y2_copy(way).wait_recv()
        for k in range(2):
            total = wt[y, k].astype(f32) + yr2[k].astype(f32) + yl2[k].astype(f32)
            gd[:, k * wid : (k + 1) * wid] = total
    else:
        y_term(y)
        for k in range(2):
            gd[:, k * wid : (k + 1) * wid] = wt[y, k].astype(f32)

    for r in range(1, nh):
        f_copy(r).wait_recv()
    total = zs[nz - 1, :, own].astype(f32)
    for r in range(nh - 1):
        total = total + far[r].astype(f32)
    total = total.astype(bf16)
    for a, ref in enumerate((out_m, out_g)):
        last = jnp.zeros((SLOT, LANES), f32)
        for g in range(groups):
            lanes = total[a][:, g * LANES : (g + 1) * LANES]
            ref[:, g * LANES : (g + 1) * LANES] = lanes[:tok]
            last = last + mm(grow_one[g], lanes)
        ref[:, main:] = last[:tok].astype(bf16)

    for cp in (*h_out, *hp_out):
        cp.wait_send()
    for k in range(3):
        p_copy(k).wait_send()
    p_sib().wait_send()
    for r in range(1, nh):
        f_copy(r).wait_send()
    if ny > 1:
        for way in range(2):
            y1_copy(way).wait_send()
            y2_copy(way).wait_send()

    def z_drain(r, carry):
        for d in range(half):
            z_copy(0, r, d).wait_send()
        for d in range(half - 1):
            z_copy(1, r, d).wait_send()
        return carry

    for way in range(2):
        zz_copy(way, 0, True).wait_send()
        for m in range(1, half):
            zz_copy(way, m, False).wait_send()

    def sum_drain(k, carry):
        for way in range(2):
            x1_copy(k, way).wait_send()
            x2_copy(k, way).wait_send()
        cs_copy(k).wait_send()
        return carry

    lax.fori_loop(0, nz, sum_drain, 0)

    def drain(u, carry):
        for way in range(2):
            xa_copy(u, way).wait_send()
        xb_copy(u, 0).wait_send()
        sib_copy(u).wait_send()
        return carry

    lax.fori_loop(0, nh, z_drain, 0)
    lax.fori_loop(0, items, drain, 0)


def selections(tok, groups):
    one = np.zeros((groups, SLOT, SLOT), np.float32)
    for i in range(tok):
        one[i // 4, i, tok + i % 4] = 1
    return tuple(jnp.asarray(a, bf16) for a in (one, one.transpose(0, 2, 1)))


def fused(tokens, grad_out, ids, probs, wg, wu, wd, ny, nh, nz, tok):
    hid, width = wg.shape
    wid = width // nz
    main = wid - LANES
    rows = nh * SLOT
    every = NX * NC * rows
    half = nz // 2
    items = nh * nz
    vmem, dma = pltpu.VMEM, pltpu.SemaphoreType.DMA
    block = (2, SLOT, main)
    scratch = [
        vmem((SLOT, wid), bf16),
        vmem((NX, NC, rows, LANES), bf16),
        vmem((nz, 2, NX, NC, rows, main), bf16),
        vmem((nz, every, LANES), bf16),
        vmem((hid, width), bf16),
        vmem((hid, width), bf16),
        vmem((hid, width), bf16),
        vmem((every, hid), f32),
        vmem((every, hid), f32),
        vmem((every, hid), f32),
        vmem((every, LANES), f32),
        vmem((every, hid), bf16),
        vmem((every, hid), bf16),
        vmem((every, hid), bf16),
        vmem((nz, 2, NX, NC, rows, main), bf16),
        vmem((nz, 2, NX, rows, main), bf16),
        vmem((nz, rows, main), bf16),
        vmem((nz, rows, main), bf16),
        vmem((nz, 2, rows, main), bf16),
        vmem((nz, 2, rows, main), bf16),
        vmem((nz, 2, rows, main), bf16),
        vmem((half, 2, rows, main), bf16),
        vmem((half, 2, rows, main), bf16),
        vmem((nz // 2, 2, hid, wid), bf16),
        vmem((hid, wid), bf16),
        vmem((hid, wid), bf16),
        vmem((2, hid, wid), bf16),
        vmem((2, hid, wid), bf16),
        vmem((max(nh - 1, 1), *block), bf16),
        dma((3,)),
        *[dma((nh,))] * 4,
        *[dma((4,))] * 2,
        *[dma((2, nh * half))] * 2,
        *[dma((2, items))] * 2,
        *[dma((items,))] * 2,
        *[dma((items,))] * 2,
        *[dma((nz,))] * 2,
        *[dma((2, nz))] * 2,
        *[dma((2, nz))] * 2,
        *[dma((2, half))] * 2,
        *[dma((4,))] * 2,
        *[dma((nh,))] * 2,
    ]
    in_vmem, anywhere = pl.BlockSpec(memory_space=pltpu.VMEM), pl.BlockSpec(memory_space=pl.ANY)
    return pl.pallas_call(
        functools.partial(kernel, ny, nh, nz, tok, wid),
        out_shape=(
            jax.ShapeDtypeStruct((tok, wid), bf16),
            jax.ShapeDtypeStruct((tok, wid), bf16),
            jax.ShapeDtypeStruct((hid, 2 * wid), f32),
        ),
        in_specs=[in_vmem] * 6 + [anywhere] * 3,
        out_specs=(in_vmem, in_vmem, in_vmem),
        scratch_shapes=scratch,
        compiler_params=pltpu.CompilerParams(
            collective_id=0, has_side_effects=True, vmem_limit_bytes=VMEM_BYTES
        ),
        cost_estimate=pl.CostEstimate(
            flops=14 * every * width * hid, bytes_accessed=6 * width * hid, transcendentals=every * hid
        ),
    )(tokens, grad_out, ids, probs, *selections(tok, main // LANES), wg, wu, wd)


def on_device(tokens, grad_out, route_ids, route_probs, w_gate, w_up, w_down):
    tok, wid = tokens.shape
    ny, nz = lax.axis_size("dp"), lax.axis_size("tensor")
    nh = lax.axis_size("expert") // (NX * NC)
    ids, probs = (jnp.pad(a.T, ((0, 0), (0, LANES - tok))) for a in (route_ids, route_probs))
    mixed, grad_tokens, grad_down = fused(
        tokens, grad_out, ids, probs, w_gate[0].T, w_up[0].T, w_down[0], ny, nh, nz, tok
    )
    return (mixed, grad_tokens, grad_down[None])


def solution(mesh):
    return jax.shard_map(
        on_device,
        mesh=mesh,
        in_specs=(
            P(("dp", "expert"), "tensor"),
            P(("dp", "expert"), "tensor"),
            P(("dp", "expert"), None),
            P(("dp", "expert"), None),
            P("expert", None, "tensor"),
            P("expert", None, "tensor"),
            P("expert", "tensor", None),
        ),
        out_specs=(
            P(("dp", "expert"), "tensor"),
            P(("dp", "expert"), "tensor"),
            P("expert", "tensor", "dp"),
        ),
        check_vma=False,
    )
```

time: 145 us -> 142 us (0.979)
  Pallas kernels: 136 us -> 134 us
    pallas_call x1, Pallas kernels: 136 us -> 134 us  [fused(): pl.pallas_call(functools.partial(kernel, ny, nh, nz, tok, wid), out_shape...]
where the time goes in v4:
time: 142 us
  Pallas kernels  134 us (94%)
  local copies, waits for them, and re-layouts  7.3 us (5%)
    pallas_call x1, Pallas kernels, fused(): pl.pallas_call(functools.partial(kernel, ny, nh, nz, tok, wid), out_shape...  134 us
    unnamed x3, local copies, waits for them, and re-layouts  4.73 us

profile of v4, /device:TPU:24, one launch (start us, length us, event | category | flops | bytes accessed | tf_op | source)
XLA Modules:
  0.0 141.9 jit_solution(14096806001324146585)
XLA Ops:
  0.6 1.3 pad.8.ids_in
  1.9 1.3 pad.9.probs_in
  3.2 133.9 %shard_map.112 = (bf16[12,512]{1,0:T(8,128)(2,1)}, bf16[12,512]{1,0:T(8,128)(2,1)}, f32[192,1024]{1,0:T(8,128)}) custom-call(bf16[12,512]{1,0:T(8,128)(2,1)} %tok_in.1, bf16[12,512]{1,0:T(8,128)(2,1)} %go_in.1, s32[8,128]{1,0:T(8,128)} %pad.8.ids_in, f32[8,128]{1,0:T(8,128)} %pad.9.probs_in, bf16[3,16,16]{2,1,0:T(8,128)(2,1)} %constant.8.clone.grow_one, ...), custom_call_target="tpu_custom_call" | custom-call | flops 5637144576 | bytes 4718592 | tf_op jit(solution)/shard_map/pallas_call | solution.py:585
  137.2 1.3 copy.15
  138.5 1.3 copy.16
  139.8 2.1 %copy.17 = f32[1,192,1024]{2,1,0:T(8,128)} copy(f32[1,192,1024]{2,1,0:T(8,128)} %bitcast.10) | data formatting | bytes 1572864
